TPU v7x, 1024 devices: a whole 8x8x8 slice. The times are simulated.
1024 devices in a mesh: dp: 16 (over z, core), proto: 64 (over y, x).
Axes of the slice: x: 8, y: 8, z: 8, core: 2. Of those that a mesh axis runs over, the one named last changes fastest.
Arguments:
- student_feat: bfloat16 [12288, 256], P(('dp', 'proto'))
- teacher_feat: bfloat16 [12288, 256], P(('dp', 'proto'))
- prototypes: bfloat16 [65536, 256], P('proto')
- teacher_prototypes: bfloat16 [65536, 256], P('proto')
- live_count: int32 [16], replicated, may hold values from 192 to 768, as said below
Outputs:
- student_grad: float32 [12288, 256], P(('dp', 'proto'))
- proto_grad: float32 [64, 1024, 256], P('proto', 'dp')
Inputs may be any that keep to these rules, and one draw needn't show every extreme that they name: `live_count`: some group is full (768 live rows) in every draw; live rows are the first ones of each group.
All inputs are finite; a program needn't handle non-finite values.
Results may differ from a plain program's by a relative error of at most 0.0026.
Values may be sent and summed in bfloat16 or wider, within the bound.
A program may use at most 32 MiB of HBM per device.

v0:
```python
import jax
import jax.numpy as jnp
from jax import lax
from jax.sharding import PartitionSpec as P

ITERS = 3


student_temp = 0.1
teacher_temp = 0.07
eps_norm = 1e-06


def unit_rows(values):
    widened = values.astype(jnp.float32)
    length = jnp.sqrt(jnp.sum(widened * widened, axis=1, keepdims=True) + eps_norm)
    return (widened / length, length)


def sample_totals(values):
    return lax.psum(values, "proto")


def proto_totals(values):
    return lax.psum(values, "dp")


def on_device(student_feat, teacher_feat, prototypes, teacher_prototypes, live_count):
    student_unit, student_length = unit_rows(student_feat)
    teacher_unit, teacher_length = unit_rows(teacher_feat)
    proto_unit, proto_length = unit_rows(prototypes)
    teacher_proto, teacher_proto_length = unit_rows(teacher_prototypes)
    proto_bf = proto_unit.astype(jnp.bfloat16)
    teacher_proto_bf = teacher_proto.astype(jnp.bfloat16)
    student_rows, teacher_rows = (
        lax.all_gather(student_unit.astype(jnp.bfloat16), "proto", axis=0, tiled=True),
        lax.all_gather(teacher_unit.astype(jnp.bfloat16), "proto", axis=0, tiled=True),
    )
    group_size = student_rows.shape[0]
    live_rows = live_count[lax.axis_index("dp")]
    live_mask = jnp.arange(group_size, dtype=jnp.int32) < live_rows
    live_column = live_mask[:, None]
    contract_last = (((1,), (1,)), ((), ()))
    logits = (
        lax.dot_general(student_rows, proto_bf, contract_last, preferred_element_type=jnp.float32)
        / student_temp
    )
    teacher_scores = (
        lax.dot_general(
            teacher_rows, teacher_proto_bf, contract_last, preferred_element_type=jnp.float32
        )
        / teacher_temp
    )
    weights = jnp.where(live_column, jnp.exp(teacher_scores), 0.0)
    partition = sample_totals(jnp.sum(jnp.exp(logits), axis=1))
    targets = weights
    for iteration in range(ITERS):
        targets = targets / proto_totals(jnp.sum(targets, axis=0))[None, :]
        row_sums = sample_totals(jnp.sum(targets, axis=1))
        targets = targets / jnp.where(live_mask, row_sums, 1.0)[:, None]
    student_probs = jnp.exp(logits - jnp.log(partition)[:, None])
    grad_logits = jnp.where(live_column, (student_probs - targets) / student_temp, 0.0).astype(
        jnp.bfloat16
    )
    grad_block = grad_logits
    pulled = lax.psum_scatter(
        jnp.dot(grad_block, proto_bf, preferred_element_type=jnp.float32),
        "proto",
        scatter_dimension=0,
        tiled=True,
    )
    student_grad = (
        pulled - student_unit * jnp.sum(student_unit * pulled, axis=1, keepdims=True)
    ) / student_length
    own_protos = prototypes.shape[0] // lax.axis_size("dp")
    contract_first = (((0,), (0,)), ((), ()))
    grad_block = grad_logits
    pushed = lax.psum_scatter(
        lax.dot_general(
            grad_block, student_rows, contract_first, preferred_element_type=jnp.float32
        ),
        "dp",
        scatter_dimension=0,
        tiled=True,
    )
    first_proto = lax.axis_index("dp") * own_protos
    own_units = lax.dynamic_slice_in_dim(proto_unit, first_proto, own_protos, 0)
    own_lengths = lax.dynamic_slice_in_dim(proto_length, first_proto, own_protos, 0)
    proto_grad = (
        pushed - own_units * jnp.sum(own_units * pushed, axis=1, keepdims=True)
    ) / own_lengths
    return (student_grad, proto_grad[None])


def solution(mesh):
    return jax.shard_map(
        on_device,
        mesh=mesh,
        in_specs=(
            P(("dp", "proto"), None),
            P(("dp", "proto"), None),
            P("proto", None),
            P("proto", None),
            P(),
        ),
        out_specs=(P(("dp", "proto"), None), P("proto", "dp", None)),
        check_vma=False,
    )
```

profile of v0, /device:TPU:1, one launch (start us, length us, event | category | flops | bytes accessed | tf_op | source)
XLA Modules:
  0.0 770.9 jit_solution(1857139292804292204)
XLA Ops:
  10.8 40.3 %all-gather.1 = bf16[64,12,256]{2,1,0:T(8,128)(2,1)S(1)} all-gather(bf16[1,12,256]{2,1,0:T(8,128)(2,1)S(1)} %fusion.26), channel_id=1, replica_groups=mesh['dp'=16,'proto'=64] {'proto'}, dimensions={0}, use_global_device_ids=true | all-gather | bytes 399360 | tf_op jit(solution)/shard_map/all_gather | solution.py:37
  52.5 2.0 fusion.30
  54.5 48.2 %psum.50 = f32[1024]{0:T(1024)S(1)} all-reduce(f32[1024]{0:T(1024)S(1)} %get-tuple-element.4), channel_id=1, replica_groups=mesh['dp'=16,'proto'=64] {'dp'}, use_global_device_ids=true, to_apply=%region_7.8 | all-reduce | flops 1024 | bytes 8192 | tf_op jit(solution)/shard_map/psum | solution.py:25
  103.0 113.1 %psum.51 = f32[768]{0:T(1024)S(1)} all-reduce(f32[768]{0:T(1024)S(1)} %divide_reduce_fusion), channel_id=1, replica_groups=mesh['dp'=16,'proto'=64] {'proto'}, use_global_device_ids=true, to_apply=%region_9.10 | all-reduce | flops 768 | bytes 6144 | tf_op jit(solution)/shard_map/psum | solution.py:21
  217.3 50.6 %psum.52 = f32[1024]{0:T(1024)S(1)} all-reduce(f32[1024]{0:T(1024)S(1)} %fusion.10), channel_id=1, replica_groups=mesh['dp'=16,'proto'=64] {'dp'}, use_global_device_ids=true, to_apply=%region_11.12 | all-reduce | flops 1024 | bytes 8192 | tf_op jit(solution)/shard_map/psum | solution.py:25
  268.6 110.2 %psum.53 = f32[768]{0:T(1024)S(1)} all-reduce(f32[768]{0:T(1024)S(1)} %fusion.11), channel_id=1, replica_groups=mesh['dp'=16,'proto'=64] {'proto'}, use_global_device_ids=true, to_apply=%region_13.14 | all-reduce | flops 768 | bytes 6144 | tf_op jit(solution)/shard_map/psum | solution.py:21
  380.2 51.3 %psum.54 = f32[1024]{0:T(1024)S(1)} all-reduce(f32[1024]{0:T(1024)S(1)} %fusion.12), channel_id=1, replica_groups=mesh['dp'=16,'proto'=64] {'dp'}, use_global_device_ids=true, to_apply=%region_15.16 | all-reduce | flops 1024 | bytes 8192 | tf_op jit(solution)/shard_map/psum | solution.py:25
  431.6 1.6 fusion.13
  433.8 40.8 %all-gather = bf16[64,12,256]{2,1,0:T(8,128)(2,1)} all-gather(bf16[1,12,256]{2,1,0:T(8,128)(2,1)S(1)} %convert_bitcast_fusion), channel_id=1, replica_groups=mesh['dp'=16,'proto'=64] {'proto'}, dimensions={0}, use_global_device_ids=true | all-gather | bytes 399360 | tf_op jit(solution)/shard_map/all_gather | solution.py:36
  477.0 4.0 exponential_reduce_fusion
  481.0 115.8 %all-reduce.2 = (f32[768]{0:T(1024)}, f32[768]{0:T(1024)}) all-reduce(f32[768]{0:T(1024)} %fusion.13, f32[768]{0:T(1024)} %get-tuple-element.6), channel_id=1, replica_groups=mesh['dp'=16,'proto'=64] {'proto'}, use_global_device_ids=true, to_apply=%region_17.18 | all-reduce | flops 1536 | bytes 12288 | tf_op jit(solution)/shard_map/psum | solution.py:21
  596.8 1.4 fusion.27
  598.9 3.3 select_convert_fusion
  603.3 1.6 fusion.31
  604.9 2.1 fusion.19
  607.1 97.4 %fusion = f32[16,256]{1,0:T(8,128)S(1)} fusion(f32[768,256]{1,0:T(8,128)S(1)} %fusion.19), kind=kCustom, calls=%all-reduce-scatter | all-reduce-scatter fusion | flops 262145 | bytes 806912
  704.5 2.6 collective-permute-start.15
  707.2 2.6 collective-permute-start
  709.8 3.2 collective-permute-start.1
  713.0 5.0 collective-permute-start.10
  718.1 5.8 collective-permute-start.11
  723.9 3.8 collective-permute-start.12
  727.8 4.2 collective-permute-start.13
  733.3 3.1 collective-permute-start.2
  736.4 5.7 collective-permute-start.3
  742.2 2.5 collective-permute-start.4
  744.7 4.0 collective-permute-start.5
  750.1 2.2 collective-permute-start.7
  752.3 2.8 collective-permute-start.8
  755.1 1.4 collective-permute-start.9
  758.8 1.8 concatenate
  762.5 1.6 divide_bitcast_fusion
  (71 shorter events, 19.5 us)
Async XLA Ops:
  7.2 754.4 %reduce-scatter.4.cloned.1.call-start = ((), (), s32[]{:S(2)}) async-start(), calls=%async_computation.1 | async-start | bytes 1114112 | tf_op jit(solution)/shard_map/reduce_scatter | solution.py:78
  9.2 45.2 %copy-start.10 = (pred[768]{0:T(1024)(128)(4,1)}, pred[768]{0:T(1024)(128)(4,1)S(1)}, u32[]{:S(2)}) copy-start(pred[768]{0:T(1024)(128)(4,1)S(1)} %iota_compare_fusion) | copy-start | bytes 2308
  267.9 163.7 %copy-start.3 = (f32[1024]{0:T(1024)}, f32[1024]{0:T(1024)S(1)}, u32[]{:S(2)}) copy-start(f32[1024]{0:T(1024)S(1)} %psum.52) | copy-start | bytes 12292
  379.5 53.6 %copy-start.4 = (f32[768]{0:T(1024)}, f32[768]{0:T(1024)S(1)}, u32[]{:S(2)}) copy-start(f32[768]{0:T(1024)S(1)} %fusion.28) | copy-start | bytes 9220
  379.5 53.6 %copy-start.2 = (bf16[12,256]{1,0:T(8,128)(2,1)S(1)}, bf16[12,256]{1,0:T(8,128)(2,1)}, u32[]{:S(2)}) copy-start(bf16[12,256]{1,0:T(8,128)(2,1)} %param.5) | copy-start | bytes 18436
  431.5 1.8 copy-start.5
  433.2 0.6 copy-start.8
  477.0 4.0 copy-start.6
  602.1 1.2 copy-start.1
  603.3 1.6 copy-start
  603.3 1.6 copy-start.7
  604.9 155.7 %copy-start.9 = (f32[12]{0:T(128)S(1)}, f32[12]{0:T(128)}, u32[]{:S(2)}) copy-start(f32[12]{0:T(128)} %copy-done.8) | copy-start | bytes 148
  704.5 19.4 %collective-permute-start.15 = (f32[12,256]{1,0:T(8,128)S(1)}, f32[12,256]{1,0:T(8,128)S(1)}, u32[]{:S(2)}, u32[]{:S(2)}) collective-permute-start(f32[12,256]{1,0:T(8,128)S(1)} %slice), channel_id=1, source_target_pairs={{0,16},{1,17},{2,18},{3,19},{4,20},{5,21},{6,22},{7,23},{8,24},{9,... | collective-permute-start | bytes 36872
  707.2 20.6 %collective-permute-start = (f32[16,256]{1,0:T(8,128)S(1)}, f32[16,256]{1,0:T(8,128)S(1)}, u32[]{:S(2)}, u32[]{:S(2)}) collective-permute-start(f32[16,256]{1,0:T(8,128)S(1)} %fusion), channel_id=1, source_target_pairs={{0,1},{1,2},{2,3},{3,4},{4,5},{5,6},{6,7},{7,8},{8,9},{9,10},{10,1... | collective-permute-start | bytes 49160
  709.8 22.2 %collective-permute-start.1 = (f32[16,256]{1,0:T(8,128)S(1)}, f32[16,256]{1,0:T(8,128)S(1)}, u32[]{:S(2)}, u32[]{:S(2)}) collective-permute-start(f32[16,256]{1,0:T(8,128)S(1)} %fusion), channel_id=1, source_target_pairs={{0,2},{1,3},{2,4},{3,5},{4,6},{5,7},{6,8},{7,9},{8,10},{9,11},{10,... | collective-permute-start | bytes 49160
  713.0 20.2 %collective-permute-start.10 = (f32[16,256]{1,0:T(8,128)S(1)}, f32[16,256]{1,0:T(8,128)S(1)}, u32[]{:S(2)}, u32[]{:S(2)}) collective-permute-start(f32[16,256]{1,0:T(8,128)S(1)} %fusion), channel_id=1, source_target_pairs={{0,11},{1,12},{2,13},{3,14},{4,15},{5,16},{6,17},{7,18},{8,19},{9,... | collective-permute-start | bytes 49160
  718.1 18.3 %collective-permute-start.11 = (f32[16,256]{1,0:T(8,128)S(1)}, f32[16,256]{1,0:T(8,128)S(1)}, u32[]{:S(2)}, u32[]{:S(2)}) collective-permute-start(f32[16,256]{1,0:T(8,128)S(1)} %fusion), channel_id=1, source_target_pairs={{0,12},{1,13},{2,14},{3,15},{4,16},{5,17},{6,18},{7,19},{8,20},{9,... | collective-permute-start | bytes 49160
  723.9 18.2 %collective-permute-start.12 = (f32[16,256]{1,0:T(8,128)S(1)}, f32[16,256]{1,0:T(8,128)S(1)}, u32[]{:S(2)}, u32[]{:S(2)}) collective-permute-start(f32[16,256]{1,0:T(8,128)S(1)} %fusion), channel_id=1, source_target_pairs={{0,13},{1,14},{2,15},{3,16},{4,17},{5,18},{6,19},{7,20},{8,21},{9,... | collective-permute-start | bytes 49160
  727.8 16.9 %collective-permute-start.13 = (f32[16,256]{1,0:T(8,128)S(1)}, f32[16,256]{1,0:T(8,128)S(1)}, u32[]{:S(2)}, u32[]{:S(2)}) collective-permute-start(f32[16,256]{1,0:T(8,128)S(1)} %fusion), channel_id=1, source_target_pairs={{0,14},{1,15},{2,16},{3,17},{4,18},{5,19},{6,20},{7,21},{8,22},{9,... | collective-permute-start | bytes 49160
  732.0 16.8 %collective-permute-start.14 = (f32[16,256]{1,0:T(8,128)S(1)}, f32[16,256]{1,0:T(8,128)S(1)}, u32[]{:S(2)}, u32[]{:S(2)}) collective-permute-start(f32[16,256]{1,0:T(8,128)S(1)} %fusion), channel_id=1, source_target_pairs={{0,15},{1,16},{2,17},{3,18},{4,19},{5,20},{6,21},{7,22},{8,23},{9,... | collective-permute-start | bytes 49160
  733.3 16.8 %collective-permute-start.2 = (f32[16,256]{1,0:T(8,128)S(1)}, f32[16,256]{1,0:T(8,128)S(1)}, u32[]{:S(2)}, u32[]{:S(2)}) collective-permute-start(f32[16,256]{1,0:T(8,128)S(1)} %fusion), channel_id=1, source_target_pairs={{0,3},{1,4},{2,5},{3,6},{4,7},{5,8},{6,9},{7,10},{8,11},{9,12},{10... | collective-permute-start | bytes 49160
  736.4 15.9 %collective-permute-start.3 = (f32[16,256]{1,0:T(8,128)S(1)}, f32[16,256]{1,0:T(8,128)S(1)}, u32[]{:S(2)}, u32[]{:S(2)}) collective-permute-start(f32[16,256]{1,0:T(8,128)S(1)} %fusion), channel_id=1, source_target_pairs={{0,4},{1,5},{2,6},{3,7},{4,8},{5,9},{6,10},{7,11},{8,12},{9,13},{1... | collective-permute-start | bytes 49160
  742.2 13.0 %collective-permute-start.4 = (f32[16,256]{1,0:T(8,128)S(1)}, f32[16,256]{1,0:T(8,128)S(1)}, u32[]{:S(2)}, u32[]{:S(2)}) collective-permute-start(f32[16,256]{1,0:T(8,128)S(1)} %fusion), channel_id=1, source_target_pairs={{0,5},{1,6},{2,7},{3,8},{4,9},{5,10},{6,11},{7,12},{8,13},{9,14},{... | collective-permute-start | bytes 49160
  744.7 14.0 %collective-permute-start.5 = (f32[16,256]{1,0:T(8,128)S(1)}, f32[16,256]{1,0:T(8,128)S(1)}, u32[]{:S(2)}, u32[]{:S(2)}) collective-permute-start(f32[16,256]{1,0:T(8,128)S(1)} %fusion), channel_id=1, source_target_pairs={{0,6},{1,7},{2,8},{3,9},{4,10},{5,11},{6,12},{7,13},{8,14},{9,15},... | collective-permute-start | bytes 49160
  748.8 10.0 %collective-permute-start.6 = (f32[16,256]{1,0:T(8,128)S(1)}, f32[16,256]{1,0:T(8,128)S(1)}, u32[]{:S(2)}, u32[]{:S(2)}) collective-permute-start(f32[16,256]{1,0:T(8,128)S(1)} %fusion), channel_id=1, source_target_pairs={{0,7},{1,8},{2,9},{3,10},{4,11},{5,12},{6,13},{7,14},{8,15},{9,16}... | collective-permute-start | bytes 49160
  750.1 8.7 %collective-permute-start.7 = (f32[16,256]{1,0:T(8,128)S(1)}, f32[16,256]{1,0:T(8,128)S(1)}, u32[]{:S(2)}, u32[]{:S(2)}) collective-permute-start(f32[16,256]{1,0:T(8,128)S(1)} %fusion), channel_id=1, source_target_pairs={{0,8},{1,9},{2,10},{3,11},{4,12},{5,13},{6,14},{7,15},{8,16},{9,17... | collective-permute-start | bytes 49160
  752.3 6.5 collective-permute-start.8
  755.1 3.7 collective-permute-start.9
Sparse Core Ops, SparseCore 0:
  605.0 90.2 reduce-scatter.3
where the time goes:
time: 783 us; the launch traced here: 771 us
  blocking collectives  668 us (85%)
  starting transfers between devices  51.8 us (7%)
  other arithmetic  18.4 us (2%)
  between operations  15.2 us (2%)
  matrix products  9.67 us (1%)
  local copies, waits for them, and re-layouts  8.1 us (1%)
    psum x3, blocking collectives, sample_totals(): return lax.psum(values, 'proto')  339 us
    psum x3, blocking collectives, proto_totals(): return lax.psum(values, 'dp')  150 us
    unnamed x1, blocking collectives  97.4 us
    unnamed x16, starting transfers between devices  51.8 us
    all_gather x1, blocking collectives, on_device(): lax.all_gather(student_unit.astype(jnp.bfloat16), 'proto', axis=0, tiled=...  40.8 us
    all_gather x1, blocking collectives, on_device(): lax.all_gather(teacher_unit.astype(jnp.bfloat16), 'proto', axis=0, tiled=...  40.3 us
  transfers between devices with their start and end apart: 17, of which 0 were waited for; matrix products, arithmetic and copies ran while one was open for 13% of the time, Pallas kernels for 0%

commit v1 on v0

v1 whole, which is shorter than its diff:
```python
import jax
import jax.numpy as jnp
from jax import lax
from jax.experimental import pallas as pl
from jax.experimental.pallas import tpu as pltpu
from jax.sharding import PartitionSpec as P

MESH = pl.DeviceIdType.MESH
F32 = jnp.float32
BF16 = jnp.bfloat16

ITERS = 3
EPS = 1e-06
NX = 8
SLOT = 12
HALF = 6
CHUNK = NX * HALF
ROWS = 768
PROTOS = 1024
D = 256
NT = (((1,), (1,)), ((), ()))
TN = (((0,), (0,)), ((), ()))
FAR_FIRST = (4, 3, 5, 2, 6, 1, 7)


def unit_rows(values):
    widened = values.astype(F32)
    length = jnp.sqrt(jnp.sum(widened * widened, axis=1, keepdims=True) + EPS)
    return widened * (1.0 / length), length


def slot_row(index):
    first = index + HALF * ((index * 10923) >> 16)
    rest = index - ROWS // 2
    block = (rest * 1366) >> 16
    inner = rest - block * CHUNK
    six = (inner * 43) >> 8
    second = six * (NX * SLOT) + block * SLOT + HALF + inner - six * HALF
    return jnp.where(index < ROWS // 2, first, second)


def kernel(
    sf, tf, pr, tp, lc, out_s, out_p,
    stage, msg, g1, trow, srow, tpb, prb, wt, ex, gr, ub, ab,
    cs, cr, rs, rr, ps, pg, vv,
    pull, pullb, q1, q2s, q2, push, pushb, sib, zsend, zrecv,
    gsend, grecv, csend, crecv, rsend, rrecv, psend, precv, fsend, frecv,
):
    d = lax.axis_index("dp")
    p = lax.axis_index("proto")
    y, x = p // NX, p % NX
    z, c = d // 2, d % 2

    def xp(k):
        return (d, y * NX + (x + k) % NX)

    def yp(k):
        return (d, ((y + k) % NX) * NX + x)

    def dpp(k):
        return ((d + k) % 16, p)

    def send(src, dst, ssem, rsem, dev):
        pltpu.make_async_remote_copy(
            src_ref=src, dst_ref=dst, send_sem=ssem, recv_sem=rsem, device_id=dev, device_id_type=MESH
        ).start()

    def wait(ref, sem):
        pltpu.make_async_copy(ref, ref, sem).wait()

    barrier = pltpu.get_barrier_semaphore()
    for k in range(1, NX):
        pl.semaphore_signal(barrier, inc=1, device_id=xp(k), device_id_type=MESH)
        pl.semaphore_signal(barrier, inc=1, device_id=yp(k), device_id_type=MESH)
    for k in range(1, 16):
        pl.semaphore_signal(barrier, inc=1, device_id=dpp(k), device_id_type=MESH)

    su, _ = unit_rows(sf[...])
    tu, _ = unit_rows(tf[...])
    stage[...] = jnp.zeros_like(stage)
    stage[0, 0:HALF] = tu[0:HALF]
    stage[0, HALF:SLOT] = su[0:HALF]
    stage[1, 0:HALF] = tu[HALF:SLOT]
    stage[1, HALF:SLOT] = su[HALF:SLOT]
    msg[...] = stage[...].astype(BF16)
    g1[0, x] = msg[0]
    g1[1, y] = msg[1]
    pl.semaphore_wait(barrier, 2 * (NX - 1) + 15)
    for k in FAR_FIRST:
        send(msg.at[0], g1.at[0, x], gsend.at[0], grecv.at[0], xp(k))
        send(msg.at[1], g1.at[1, y], gsend.at[1], grecv.at[1], yp(k))

    def unit_protos(i, carry):
        rows = pl.ds(pl.multiple_of(i * 128, 128), 128)
        tpb[rows, :] = unit_rows(tp[rows, :])[0].astype(BF16)
        prb[rows, :] = unit_rows(pr[rows, :])[0].astype(BF16)
        return carry

    lax.fori_loop(0, PROTOS // 128, unit_protos, 0)
    live = lc[d]
    ub[...] = (slot_row(lax.broadcasted_iota(jnp.int32, (ROWS, 128), 0)) < live).astype(F32)
    flat = lax.broadcasted_iota(jnp.int32, (8, 128), 0) * 128 + lax.broadcasted_iota(jnp.int32, (8, 128), 1)
    live_flat = (slot_row(flat) < live) & (flat < ROWS)

    ri = lax.broadcasted_iota(jnp.int32, (2 * CHUNK, NX * 16), 0)
    ci = lax.broadcasted_iota(jnp.int32, (2 * CHUNK, NX * 16), 1)
    inner = jnp.where(ri < CHUNK, ri, ri - CHUNK)
    six = (inner * 43) >> 8
    source = six * 16 + (inner - six * HALF) + jnp.where(ri < CHUNK, 0, HALF)
    pick = (ci == source).astype(F32).astype(BF16)
    first = pl.ds(pl.multiple_of(y * CHUNK, CHUNK), CHUNK)
    second = pl.ds(pl.multiple_of(ROWS // 2 + x * CHUNK, CHUNK), CHUNK)
    for half, place, peer in ((0, first, yp), (1, second, xp)):
        wait(g1.at[half, pl.ds(0, NX - 1)], grecv.at[half])
        rows = jnp.dot(pick, g1[half].reshape(NX * 16, D), preferred_element_type=F32).astype(BF16)
        trow[place, :] = rows[0:CHUNK]
        srow[place, :] = rows[CHUNK:]
        for k in FAR_FIRST:
            send(trow.at[place], trow.at[place], gsend.at[2 + half], grecv.at[2 + half], peer(k))

    def scores(rows_ref, protos_ref, out_ref, scale):
        for m in range(3):
            for n in range(4):
                rows, cols = pl.ds(m * 256, 256), pl.ds(n * 256, 256)
                s = lax.dot_general(rows_ref[rows, :], protos_ref[cols, :], NT, preferred_element_type=F32)
                out_ref[rows, cols] = jnp.exp(s * scale)

    wait(trow.at[pl.ds(0, 7 * CHUNK)], grecv.at[2])
    wait(trow.at[pl.ds(0, 7 * CHUNK)], grecv.at[3])
    for half, place, peer in ((0, first, yp), (1, second, xp)):
        for k in FAR_FIRST:
            send(srow.at[place], srow.at[place], gsend.at[4 + half], grecv.at[4 + half], peer(k))
    scores(trow, tpb, wt, 1.0 / 0.07)

    def column_pass(it):
        def body(i, acc):
            rows = pl.ds(pl.multiple_of(i * 32, 32), 32)
            w = wt[rows, :]
            u = ub[rows, :]
            for t in range(4):
                ut = jnp.concatenate([u[t * 8 : t * 8 + 8]] * 8, axis=1)
                acc = acc + w[t * 8 : t * 8 + 8] * ut
            return acc

        acc = lax.fori_loop(0, ROWS // 32, body, jnp.zeros((8, PROTOS), F32), unroll=4)
        total = jnp.sum(acc, axis=0, keepdims=True)
        for n in range(8):
            cs[it, n : n + 1, :] = total[:, n * 128 : n * 128 + 128]
        for k in (8, 7, 9, 6, 10, 5, 11, 4, 12, 3, 13, 2, 14, 1, 15):
            send(cs.at[it], cr.at[it, k - 1], csend.at[it], crecv.at[it], dpp(k))

    def column_wait(it):
        wait(cr.at[it], crecv.at[it])
        vv[...] = 1.0 / (cs[it] + jnp.sum(cr[it], axis=0))

    def lane_sums(src_ref, weights, out_ref):
        out_ref[...] = jnp.zeros_like(out_ref)
        for n in range(6):
            rows = pl.ds(n * 128, 128)
            acc = jnp.zeros((128, 128), F32)
            for t in range(8):
                acc = acc + src_ref[rows, pl.ds(t * 128, 128)] * weights[t : t + 1, :]
            out_ref[n : n + 1, :] = jnp.sum(acc.T, axis=0, keepdims=True)

    def spread(flat_rows, out_ref):
        for n in range(6):
            out_ref[pl.ds(n * 128, 128), :] = jnp.broadcast_to(flat_rows[n : n + 1, :], (128, 128)).T

    def proto_send(src, dst, ssem, rsem, axis):
        for k in FAR_FIRST:
            send(src.at[axis], dst.at[axis, k - 1], ssem.at[axis], rsem.at[axis], (xp, yp)[axis](k))

    def proto_sum(src, dst, rsem, axis):
        wait(dst.at[axis], rsem.at[axis])
        return src[axis] + jnp.sum(dst[axis], axis=0)

    def inverse(total):
        return jnp.where(live_flat, 1.0 / jnp.where(live_flat, total, 1.0), 0.0)

    for it in range(ITERS):
        column_pass(it)
        if it == 1:
            wait(srow.at[pl.ds(0, 7 * CHUNK)], grecv.at[4])
            wait(srow.at[pl.ds(0, 7 * CHUNK)], grecv.at[5])
            scores(srow, prb, ex, 10.0)
            lane_sums(ex, jnp.ones((8, 128), F32), ps.at[0])
            proto_send(ps, pg, psend, precv, 0)
        if it == 2:
            ps[1] = proto_sum(ps, pg, precv, 0)
            proto_send(ps, pg, psend, precv, 1)
        column_wait(it)
        src, dst, ssem, rsem = rs.at[it], rr.at[it], rsend.at[it], rrecv.at[it]
        lane_sums(wt, vv[...], src.at[0])
        proto_send(src, dst, ssem, rsem, 0)
        if it == 2:
            partition = proto_sum(ps, pg, precv, 1)
            spread(10.0 * inverse(partition), ab)

            def fold(i, carry):
                rows = pl.ds(pl.multiple_of(i * 32, 32), 32)
                a = ab[rows, :]
                for n in range(8):
                    cols = pl.ds(n * 128, 128)
                    ex[rows, cols] = ex[rows, cols] * a
                    wt[rows, cols] = wt[rows, cols] * vv[n : n + 1, :]
                return carry

            lax.fori_loop(0, ROWS // 32, fold, 0)
        rs[it, 1] = proto_sum(src, dst, rsem, 0)
        proto_send(src, dst, ssem, rsem, 1)
        total = proto_sum(src, dst, rsem, 1)
        spread(inverse(total) * (10.0 if it == ITERS - 1 else 1.0), ub)

    def grads(i, carry):
        rows = pl.ds(pl.multiple_of(i * 32, 32), 32)
        u = ub[rows, :]
        for n in range(8):
            cols = pl.ds(n * 128, 128)
            gr[rows, cols] = (ex[rows, cols] - wt[rows, cols] * u).astype(BF16)
        return carry

    lax.fori_loop(0, ROWS // 32, grads, 0)

    for m in range(3):
        rows = pl.ds(m * 256, 256)
        part = jnp.dot(gr[rows, :], prb[...], preferred_element_type=F32)
        pull[rows, :] = part
        pullb[rows, :] = part.astype(BF16)
    for k in FAR_FIRST:
        to_y = pl.ds(pl.multiple_of(((y + k) % NX) * CHUNK, CHUNK), CHUNK)
        to_x = pl.ds(pl.multiple_of(ROWS // 2 + ((x + k) % NX) * CHUNK, CHUNK), CHUNK)
        send(pullb.at[to_y], q1.at[0, k - 1], fsend.at[0], frecv.at[0], yp(k))
        send(pullb.at[to_x], q1.at[1, k - 1], fsend.at[1], frecv.at[1], xp(k))

    other = pl.ds(pl.multiple_of((1 - c) * 512, 512), 512)
    mine = pl.ds(pl.multiple_of(c * 512, 512), 512)
    pushb[...] = lax.dot_general(gr[:, other], srow[...], TN, preferred_element_type=F32).astype(BF16)
    send(pushb, sib, fsend.at[2], frecv.at[2], (z * 2 + 1 - c, p))
    push[...] = lax.dot_general(gr[:, mine], srow[...], TN, preferred_element_type=F32)
    wait(sib, frecv.at[2])
    zsend[...] = (push[...] + sib[...].astype(F32)).astype(BF16).reshape(8, 64, D)
    keeps = c == z // 4
    for i in range(8):
        to = 8 * c + (i + 2 * z + 8) % 8

        @pl.when(to != d)
        def _(to=to):
            send(zsend.at[to - 8 * c], zrecv.at[z], fsend.at[3], frecv.at[3], (to, p))

    @pl.when(keeps)
    def _():
        zrecv[z] = zsend[d - 8 * c]

    for half, own, peer in ((0, first, xp), (1, second, yp)):
        wait(q1.at[half], frecv.at[half])
        total = pull[own, :] + jnp.sum(q1[half].astype(F32), axis=0)
        for n in range(NX):
            q2s[half, n, 0:HALF] = total[n * HALF : n * HALF + HALF]
            q2s[half, n, HALF:8] = jnp.zeros((8 - HALF, D), F32)
        at = x if half == 0 else y
        for k in FAR_FIRST:
            send(q2s.at[half, (at + k) % NX], q2.at[half, k - 1], fsend.at[4 + half], frecv.at[4 + half], peer(k))

    own_rows = pl.ds(pl.multiple_of(d * 64, 64), 64)
    proto_unit, proto_length = unit_rows(pr[own_rows, :])

    @pl.when(keeps)
    def _():
        wait(zrecv.at[pl.ds(0, 7)], frecv.at[3])
        wait(zrecv.at[pl.ds(0, 7)], fsend.at[3])

    @pl.when(jnp.logical_not(keeps))
    def _():
        wait(zrecv, frecv.at[3])
        wait(zrecv, fsend.at[3])

    pushed = jnp.sum(zrecv[...].astype(F32), axis=0)
    out_p[0] = (pushed - proto_unit * jnp.sum(proto_unit * pushed, axis=1, keepdims=True)) * (1.0 / proto_length)

    student_unit, student_length = unit_rows(sf[...])
    for half in range(2):
        wait(q2.at[half], frecv.at[4 + half])
        at = x if half == 0 else y
        stage[half, 0:8] = q2s[half, at] + jnp.sum(q2[half], axis=0)
    pulled = jnp.concatenate([stage[0, 0:HALF], stage[1, 0:HALF]], axis=0)
    out_s[...] = (pulled - student_unit * jnp.sum(student_unit * pulled, axis=1, keepdims=True)) * (1.0 / student_length)

    for half in range(2):
        wait(g1.at[half, pl.ds(0, NX - 1)], gsend.at[half])
        wait(trow.at[pl.ds(0, 7 * CHUNK)], gsend.at[2 + half])
        wait(srow.at[pl.ds(0, 7 * CHUNK)], gsend.at[4 + half])
        wait(pg.at[half], psend.at[half])
        wait(q1.at[half], fsend.at[half])
        wait(q2.at[half], fsend.at[4 + half])
        for it in range(ITERS):
            wait(rr.at[it, half], rsend.at[it, half])
    for it in range(ITERS):
        wait(cr.at[it], csend.at[it])
    wait(sib, fsend.at[2])


def on_device(student_feat, teacher_feat, prototypes, teacher_prototypes, live_count):
    vmem = pl.BlockSpec(memory_space=pltpu.VMEM)
    dma = pltpu.SemaphoreType.DMA
    return pl.pallas_call(
        kernel,
        out_shape=(
            jax.ShapeDtypeStruct((SLOT, D), F32),
            jax.ShapeDtypeStruct((1, PROTOS // 16, D), F32),
        ),
        in_specs=[vmem, vmem, vmem, vmem, pl.BlockSpec(memory_space=pltpu.SMEM)],
        out_specs=(vmem, vmem),
        scratch_shapes=[
            pltpu.VMEM((2, 16, D), F32),
            pltpu.VMEM((2, 16, D), BF16),
            pltpu.VMEM((2, NX, 16, D), BF16),
            pltpu.VMEM((ROWS, D), BF16),
            pltpu.VMEM((ROWS, D), BF16),
            pltpu.VMEM((PROTOS, D), BF16),
            pltpu.VMEM((PROTOS, D), BF16),
            pltpu.VMEM((ROWS, PROTOS), F32),
            pltpu.VMEM((ROWS, PROTOS), F32),
            pltpu.VMEM((ROWS, PROTOS), BF16),
            pltpu.VMEM((ROWS, 128), F32),
            pltpu.VMEM((ROWS, 128), F32),
            pltpu.VMEM((ITERS, 8, 128), F32),
            pltpu.VMEM((ITERS, 15, 8, 128), F32),
            pltpu.VMEM((ITERS, 2, 8, 128), F32),
            pltpu.VMEM((ITERS, 2, 7, 8, 128), F32),
            pltpu.VMEM((2, 8, 128), F32),
            pltpu.VMEM((2, 7, 8, 128), F32),
            pltpu.VMEM((8, 128), F32),
            pltpu.VMEM((ROWS, D), F32),
            pltpu.VMEM((ROWS, D), BF16),
            pltpu.VMEM((2, 7, CHUNK, D), BF16),
            pltpu.VMEM((2, NX, 8, D), F32),
            pltpu.VMEM((2, 7, 8, D), F32),
            pltpu.VMEM((512, D), F32),
            pltpu.VMEM((512, D), BF16),
            pltpu.VMEM((512, D), BF16),
            pltpu.VMEM((8, 64, D), BF16),
            pltpu.VMEM((8, 64, D), BF16),
            dma((6,)),
            dma((6,)),
            dma((ITERS,)),
            dma((ITERS,)),
            dma((ITERS, 2)),
            dma((ITERS, 2)),
            dma((2,)),
            dma((2,)),
            dma((6,)),
            dma((6,)),
        ],
        compiler_params=pltpu.CompilerParams(
            collective_id=0, has_side_effects=True, vmem_limit_bytes=48 * 1024 * 1024
        ),
    )(student_feat, teacher_feat, prototypes, teacher_prototypes, live_count)


def solution(mesh):
    return jax.shard_map(
        on_device,
        mesh=mesh,
        in_specs=(
            P(("dp", "proto"), None),
            P(("dp", "proto"), None),
            P("proto", None),
            P("proto", None),
            P(),
        ),
        out_specs=(P(("dp", "proto"), None), P("proto", "dp", None)),
        check_vma=False,
    )
```

time: 783 us -> 97 us (0.12); the launches traced: 771 us -> 96.6 us
  blocking collectives: 668 us -> 0 us
  Pallas kernels: 0 us -> 90.6 us
  starting transfers between devices: 51.8 us -> 0 us
  other arithmetic: 18.4 us -> 0 us
  between operations: 15.2 us -> 0.65 us
  matrix products: 9.67 us -> 0 us
    psum x6 -> x0, blocking collectives: 489 us -> none  [the longest x3 339 us: sample_totals(): return lax.psum(values, 'proto')]
    unnamed x1 -> x0, blocking collectives: 97.4 us -> none
    pallas_call x0 -> x1, Pallas kernels: none -> 90.6 us  [on_device(): pl.pallas_call(kernel, out_shape=(jax.ShapeDtypeStruct((SLOT, D), F32), j...]
    all_gather x2 -> x0, blocking collectives: 81.1 us -> none  [the longest x1 40.8 us: on_device(): lax.all_gather(student_unit.astype(jnp.bfloat16), 'proto', axis=0, tiled=...]
    unnamed x16 -> x0, starting transfers between devices: 51.8 us -> none
    dot_general x4 -> x0, matrix products: 9.67 us -> none  [the longest x1 4.01 us: on_device(): lax.dot_general(student_rows, proto_bf, contract_last, preferred_element_...]
    reduce_sum x11 -> x0, other arithmetic: 8.34 us -> none  [the longest x4 3.43 us: unit_rows(): jnp.sum(widened * widened, axis=1, keepdims=True) + eps_norm]
  transfers between devices with their start and end apart: 17 -> 0, of which waited for: 0 -> 0; matrix products, arithmetic and copies ran while one was open for 13% -> 0% of each run, Pallas kernels for 0% -> 0%
where the time goes in v1:
time: 97 us; the launch traced here: 96.6 us
  Pallas kernels  90.6 us (93%)
  local copies, waits for them, and re-layouts  5.36 us (6%)
    pallas_call x1, Pallas kernels, on_device(): pl.pallas_call(kernel, out_shape=(jax.ShapeDtypeStruct((SLOT, D), F32), j...  90.6 us
    unnamed x12, local copies, waits for them, and re-layouts  5.36 us

profile of v1, /device:TPU:1, one launch (start us, length us, event | category | flops | bytes accessed | tf_op | source)
XLA Modules:
  0.0 96.6 jit_solution(16835152350635322736)
XLA Ops:
  0.6 0.0 copy-start
  0.6 1.0 %copy-done = bf16[1024,256]{1,0:T(8,128)(2,1)S(1)} copy-done((bf16[1024,256]{1,0:T(8,128)(2,1)S(1)}, bf16[1024,256]{1,0:T(8,128)(2,1)}, u32[]{:S(2)}) %copy-start) | copy-done | bytes 524312
  1.7 0.0 copy-start.1
  1.7 1.0 %copy-done.1 = bf16[1024,256]{1,0:T(8,128)(2,1)S(1)} copy-done((bf16[1024,256]{1,0:T(8,128)(2,1)S(1)}, bf16[1024,256]{1,0:T(8,128)(2,1)}, u32[]{:S(2)}) %copy-start.1) | copy-done | bytes 524312
  2.7 0.0 copy-start.2
  2.7 0.7 copy-done.2
  3.4 0.0 copy-start.3
  3.4 0.7 copy-done.3
  4.1 0.0 copy-start.4
  4.1 0.7 copy-done.4
  4.8 90.6 %shard_map.68 = (f32[12,256]{1,0:T(8,128)S(1)}, f32[1,64,256]{2,1,0:T(8,128)S(1)}) custom-call(bf16[12,256]{1,0:T(8,128)(2,1)S(1)} %copy-done.2, bf16[12,256]{1,0:T(8,128)(2,1)S(1)} %copy-done.3, bf16[1024,256]{1,0:T(8,128)(2,1)S(1)} %copy-done, bf16[1024,256]{1,0:T(8,128)(2,1)S(1)} %copy-done.1, s32[16]{0:T(128)S(1)} %copy-done.4), custom_call_target="tpu_custom_call" | custom-call | tf_op jit(solution)/shard_map/pallas_call | solution.py:305
  95.4 0.6 copy.9
  96.0 0.6 copy.10
Async XLA Ops:
  0.6 1.0 %copy-start = (bf16[1024,256]{1,0:T(8,128)(2,1)S(1)}, bf16[1024,256]{1,0:T(8,128)(2,1)}, u32[]{:S(2)}) copy-start(bf16[1024,256]{1,0:T(8,128)(2,1)} %pr.1) | copy-start | bytes 1572868
  1.7 1.0 %copy-start.1 = (bf16[1024,256]{1,0:T(8,128)(2,1)S(1)}, bf16[1024,256]{1,0:T(8,128)(2,1)}, u32[]{:S(2)}) copy-start(bf16[1024,256]{1,0:T(8,128)(2,1)} %tp.1) | copy-start | bytes 1572868
  2.7 0.7 copy-start.2
  3.4 0.7 copy-start.3
  4.1 0.7 copy-start.4

commit v2 on v1

--- a/solution.py
+++ b/solution.py
@@ -23,6 +23,13 @@
 FAR_FIRST = (4, 3, 5, 2, 6, 1, 7)
 
 
+def hops(k):
+    return min(k % NX, NX - k % NX) + min(k // NX, NX - k // NX)
+
+
+PLANE = sorted(range(1, NX * NX), key=lambda k: -hops(k))
+
+
 def unit_rows(values):
     widened = values.astype(F32)
     length = jnp.sqrt(jnp.sum(widened * widened, axis=1, keepdims=True) + EPS)
@@ -40,10 +47,11 @@
 
 
 def kernel(
-    sf, tf, pr, tp, lc, out_s, out_p,
+    sf_hbm, tf_hbm, pr_hbm, tp_hbm, lc_hbm, out_s, out_p,
+    sf, tf, pr, tp, lc, isem,
     stage, msg, g1, trow, srow, tpb, prb, wt, ex, gr, ub, ab,
     cs, cr, rs, rr, ps, pg, vv,
-    pull, pullb, q1, q2s, q2, push, pushb, sib, zsend, zrecv,
+    pull, pullb, q1, q2s, q2, sixes, push, pushb, sib, zsend, zrecv,
     gsend, grecv, csend, crecv, rsend, rrecv, psend, precv, fsend, frecv,
 ):
     d = lax.axis_index("dp")
@@ -57,6 +65,9 @@
     def yp(k):
         return (d, ((y + k) % NX) * NX + x)
 
+    def plane(k):
+        return (d, ((y + k // NX) % NX) * NX + (x + k % NX) % NX)
+
     def dpp(k):
         return ((d + k) % 16, p)
 
@@ -69,26 +80,40 @@
         pltpu.make_async_copy(ref, ref, sem).wait()
 
     barrier = pltpu.get_barrier_semaphore()
-    for k in range(1, NX):
-        pl.semaphore_signal(barrier, inc=1, device_id=xp(k), device_id_type=MESH)
-        pl.semaphore_signal(barrier, inc=1, device_id=yp(k), device_id_type=MESH)
+    for k in PLANE:
+        pl.semaphore_signal(barrier, inc=1, device_id=plane(k), device_id_type=MESH)
     for k in range(1, 16):
         pl.semaphore_signal(barrier, inc=1, device_id=dpp(k), device_id_type=MESH)
 
+    inputs = ((tf_hbm, tf), (sf_hbm, sf), (lc_hbm, lc), (tp_hbm, tp), (pr_hbm, pr))
+    for i, (src, dst) in enumerate(inputs):
+        pltpu.make_async_copy(src, dst, isem.at[i]).start()
+
+    def arrived(i):
+        pltpu.make_async_copy(*inputs[i], isem.at[i]).wait()
+
+    arrived(0)
+    arrived(1)
     su, _ = unit_rows(sf[...])
     tu, _ = unit_rows(tf[...])
     stage[...] = jnp.zeros_like(stage)
-    stage[0, 0:HALF] = tu[0:HALF]
-    stage[0, HALF:SLOT] = su[0:HALF]
-    stage[1, 0:HALF] = tu[HALF:SLOT]
-    stage[1, HALF:SLOT] = su[HALF:SLOT]
+    for kind, unit in enumerate((tu, su)):
+        for half in range(2):
+            six = unit[half * HALF : half * HALF + HALF]
+            stage[kind, half, 0:HALF] = six[:, 0:128]
+            stage[kind, half, HALF:SLOT] = six[:, 128:D]
     msg[...] = stage[...].astype(BF16)
-    g1[0, x] = msg[0]
-    g1[1, y] = msg[1]
-    pl.semaphore_wait(barrier, 2 * (NX - 1) + 15)
-    for k in FAR_FIRST:
-        send(msg.at[0], g1.at[0, x], gsend.at[0], grecv.at[0], xp(k))
-        send(msg.at[1], g1.at[1, y], gsend.at[1], grecv.at[1], yp(k))
+    for kind in range(2):
+        g1[kind, 0, x] = msg[kind, 0]
+        g1[kind, 1, y] = msg[kind, 1]
+    pl.semaphore_wait(barrier, NX * NX - 1 + 15)
+    for kind in range(2):
+        for k in FAR_FIRST:
+            for half, at, peer in ((0, x, xp), (1, y, yp)):
+                send(
+                    msg.at[kind, half], g1.at[kind, half, at],
+                    gsend.at[kind * 2 + half], grecv.at[kind * 2 + half], peer(k),
+                )
 
     def unit_protos(i, carry):
         rows = pl.ds(pl.multiple_of(i * 128, 128), 128)
@@ -96,11 +121,14 @@
         prb[rows, :] = unit_rows(pr[rows, :])[0].astype(BF16)
         return carry
 
+    arrived(3)
+    arrived(4)
     lax.fori_loop(0, PROTOS // 128, unit_protos, 0)
+    arrived(2)
     live = lc[d]
     ub[...] = (slot_row(lax.broadcasted_iota(jnp.int32, (ROWS, 128), 0)) < live).astype(F32)
-    flat = lax.broadcasted_iota(jnp.int32, (8, 128), 0) * 128 + lax.broadcasted_iota(jnp.int32, (8, 128), 1)
-    live_flat = (slot_row(flat) < live) & (flat < ROWS)
+    flat = lax.broadcasted_iota(jnp.int32, (6, 128), 0) * 128 + lax.broadcasted_iota(jnp.int32, (6, 128), 1)
+    live_flat = slot_row(flat) < live
 
     ri = lax.broadcasted_iota(jnp.int32, (2 * CHUNK, NX * 16), 0)
     ci = lax.broadcasted_iota(jnp.int32, (2 * CHUNK, NX * 16), 1)
@@ -110,13 +138,18 @@
     pick = (ci == source).astype(F32).astype(BF16)
     first = pl.ds(pl.multiple_of(y * CHUNK, CHUNK), CHUNK)
     second = pl.ds(pl.multiple_of(ROWS // 2 + x * CHUNK, CHUNK), CHUNK)
-    for half, place, peer in ((0, first, yp), (1, second, xp)):
-        wait(g1.at[half, pl.ds(0, NX - 1)], grecv.at[half])
-        rows = jnp.dot(pick, g1[half].reshape(NX * 16, D), preferred_element_type=F32).astype(BF16)
-        trow[place, :] = rows[0:CHUNK]
-        srow[place, :] = rows[CHUNK:]
-        for k in FAR_FIRST:
-            send(trow.at[place], trow.at[place], gsend.at[2 + half], grecv.at[2 + half], peer(k))
+
+    def second_gather(kind, rows_ref):
+        for half, place, peer in ((0, first, yp), (1, second, xp)):
+            wait(g1.at[kind, half, pl.ds(0, NX - 1)], grecv.at[kind * 2 + half])
+            picked = jnp.dot(pick, g1[kind, half].reshape(NX * 16, 128), preferred_element_type=F32).astype(BF16)
+            rows_ref[place, 0:128] = picked[0:CHUNK]
+            rows_ref[place, 128:D] = picked[CHUNK:]
+            for k in FAR_FIRST:
+                sem = 4 + kind * 2 + half
+                send(rows_ref.at[place], rows_ref.at[place], gsend.at[sem], grecv.at[sem], peer(k))
+
+    second_gather(0, trow)
 
     def scores(rows_ref, protos_ref, out_ref, scale):
         for m in range(3):
@@ -125,11 +158,9 @@
                 s = lax.dot_general(rows_ref[rows, :], protos_ref[cols, :], NT, preferred_element_type=F32)
                 out_ref[rows, cols] = jnp.exp(s * scale)
 
-    wait(trow.at[pl.ds(0, 7 * CHUNK)], grecv.at[2])
-    wait(trow.at[pl.ds(0, 7 * CHUNK)], grecv.at[3])
-    for half, place, peer in ((0, first, yp), (1, second, xp)):
-        for k in FAR_FIRST:
-            send(srow.at[place], srow.at[place], gsend.at[4 + half], grecv.at[4 + half], peer(k))
+    wait(trow.at[pl.ds(0, 7 * CHUNK)], grecv.at[4])
+    wait(trow.at[pl.ds(0, 7 * CHUNK)], grecv.at[5])
+    second_gather(1, srow)
     scores(trow, tpb, wt, 1.0 / 0.07)
 
     def column_pass(it):
@@ -154,7 +185,6 @@
         vv[...] = 1.0 / (cs[it] + jnp.sum(cr[it], axis=0))
 
     def lane_sums(src_ref, weights, out_ref):
-        out_ref[...] = jnp.zeros_like(out_ref)
         for n in range(6):
             rows = pl.ds(n * 128, 128)
             acc = jnp.zeros((128, 128), F32)
@@ -180,8 +210,8 @@
     for it in range(ITERS):
         column_pass(it)
         if it == 1:
-            wait(srow.at[pl.ds(0, 7 * CHUNK)], grecv.at[4])
-            wait(srow.at[pl.ds(0, 7 * CHUNK)], grecv.at[5])
+            wait(srow.at[pl.ds(0, 7 * CHUNK)], grecv.at[6])
+            wait(srow.at[pl.ds(0, 7 * CHUNK)], grecv.at[7])
             scores(srow, prb, ex, 10.0)
             lane_sums(ex, jnp.ones((8, 128), F32), ps.at[0])
             proto_send(ps, pg, psend, precv, 0)
@@ -189,9 +219,9 @@
             ps[1] = proto_sum(ps, pg, precv, 0)
             proto_send(ps, pg, psend, precv, 1)
         column_wait(it)
-        src, dst, ssem, rsem = rs.at[it], rr.at[it], rsend.at[it], rrecv.at[it]
-        lane_sums(wt, vv[...], src.at[0])
-        proto_send(src, dst, ssem, rsem, 0)
+        lane_sums(wt, vv[...], rs.at[it])
+        for k in PLANE:
+            send(rs.at[it], rr.at[it, k - 1], rsend.at[it], rrecv.at[it], plane(k))
         if it == 2:
             partition = proto_sum(ps, pg, precv, 1)
             spread(10.0 * inverse(partition), ab)
@@ -206,9 +236,8 @@
                 return carry
 
             lax.fori_loop(0, ROWS // 32, fold, 0)
-        rs[it, 1] = proto_sum(src, dst, rsem, 0)
-        proto_send(src, dst, ssem, rsem, 1)
-        total = proto_sum(src, dst, rsem, 1)
+        wait(rr.at[it], rrecv.at[it])
+        total = rs[it] + jnp.sum(rr[it], axis=0)
         spread(inverse(total) * (10.0 if it == ITERS - 1 else 1.0), ub)
 
     def grads(i, carry):
@@ -240,12 +269,13 @@
     wait(sib, frecv.at[2])
     zsend[...] = (push[...] + sib[...].astype(F32)).astype(BF16).reshape(8, 64, D)
     keeps = c == z // 4
-    for i in range(8):
-        to = 8 * c + (i + 2 * z + 8) % 8
-
-        @pl.when(to != d)
-        def _(to=to):
-            send(zsend.at[to - 8 * c], zrecv.at[z], fsend.at[3], frecv.at[3], (to, p))
+    for k in FAR_FIRST + (0,):
+        for core in range(2):
+            to = ((z + k) % NX) * 2 + core
+
+            @pl.when((to // 8 == c) & (to != d))
+            def _(to=to):
+                send(zsend.at[to - 8 * c], zrecv.at[z], fsend.at[3], frecv.at[3], (to, p))
 
     @pl.when(keeps)
     def _():
@@ -281,20 +311,19 @@
     for half in range(2):
         wait(q2.at[half], frecv.at[4 + half])
         at = x if half == 0 else y
-        stage[half, 0:8] = q2s[half, at] + jnp.sum(q2[half], axis=0)
-    pulled = jnp.concatenate([stage[0, 0:HALF], stage[1, 0:HALF]], axis=0)
+        sixes[half] = q2s[half, at] + jnp.sum(q2[half], axis=0)
+    pulled = jnp.concatenate([sixes[0, 0:HALF], sixes[1, 0:HALF]], axis=0)
     out_s[...] = (pulled - student_unit * jnp.sum(student_unit * pulled, axis=1, keepdims=True)) * (1.0 / student_length)
 
     for half in range(2):
-        wait(g1.at[half, pl.ds(0, NX - 1)], gsend.at[half])
-        wait(trow.at[pl.ds(0, 7 * CHUNK)], gsend.at[2 + half])
-        wait(srow.at[pl.ds(0, 7 * CHUNK)], gsend.at[4 + half])
+        for kind, rows_ref in enumerate((trow, srow)):
+            wait(g1.at[kind, half, pl.ds(0, NX - 1)], gsend.at[kind * 2 + half])
+            wait(rows_ref.at[pl.ds(0, 7 * CHUNK)], gsend.at[4 + kind * 2 + half])
         wait(pg.at[half], psend.at[half])
         wait(q1.at[half], fsend.at[half])
         wait(q2.at[half], fsend.at[4 + half])
-        for it in range(ITERS):
-            wait(rr.at[it, half], rsend.at[it, half])
     for it in range(ITERS):
+        wait(rr.at[it], rsend.at[it])
         wait(cr.at[it], csend.at[it])
     wait(sib, fsend.at[2])
 
@@ -308,12 +337,18 @@
             jax.ShapeDtypeStruct((SLOT, D), F32),
             jax.ShapeDtypeStruct((1, PROTOS // 16, D), F32),
         ),
-        in_specs=[vmem, vmem, vmem, vmem, pl.BlockSpec(memory_space=pltpu.SMEM)],
+        in_specs=[pl.BlockSpec(memory_space=pl.ANY)] * 5,
         out_specs=(vmem, vmem),
         scratch_shapes=[
-            pltpu.VMEM((2, 16, D), F32),
-            pltpu.VMEM((2, 16, D), BF16),
-            pltpu.VMEM((2, NX, 16, D), BF16),
+            pltpu.VMEM((SLOT, D), BF16),
+            pltpu.VMEM((SLOT, D), BF16),
+            pltpu.VMEM((PROTOS, D), BF16),
+            pltpu.VMEM((PROTOS, D), BF16),
+            pltpu.SMEM((16,), jnp.int32),
+            dma((5,)),
+            pltpu.VMEM((2, 2, 16, 128), F32),
+            pltpu.VMEM((2, 2, 16, 128), BF16),
+            pltpu.VMEM((2, 2, NX, 16, 128), BF16),
             pltpu.VMEM((ROWS, D), BF16),
             pltpu.VMEM((ROWS, D), BF16),
             pltpu.VMEM((PROTOS, D), BF16),
@@ -325,34 +360,35 @@
             pltpu.VMEM((ROWS, 128), F32),
             pltpu.VMEM((ITERS, 8, 128), F32),
             pltpu.VMEM((ITERS, 15, 8, 128), F32),
-            pltpu.VMEM((ITERS, 2, 8, 128), F32),
-            pltpu.VMEM((ITERS, 2, 7, 8, 128), F32),
-            pltpu.VMEM((2, 8, 128), F32),
-            pltpu.VMEM((2, 7, 8, 128), F32),
+            pltpu.VMEM((ITERS, 6, 128), F32),
+            pltpu.VMEM((ITERS, 63, 6, 128), F32),
+            pltpu.VMEM((2, 6, 128), F32),
+            pltpu.VMEM((2, 7, 6, 128), F32),
             pltpu.VMEM((8, 128), F32),
             pltpu.VMEM((ROWS, D), F32),
             pltpu.VMEM((ROWS, D), BF16),
             pltpu.VMEM((2, 7, CHUNK, D), BF16),
             pltpu.VMEM((2, NX, 8, D), F32),
             pltpu.VMEM((2, 7, 8, D), F32),
+            pltpu.VMEM((2, 8, D), F32),
             pltpu.VMEM((512, D), F32),
             pltpu.VMEM((512, D), BF16),
             pltpu.VMEM((512, D), BF16),
             pltpu.VMEM((8, 64, D), BF16),
             pltpu.VMEM((8, 64, D), BF16),
-            dma((6,)),
-            dma((6,)),
+            dma((8,)),
+            dma((8,)),
             dma((ITERS,)),
             dma((ITERS,)),
-            dma((ITERS, 2)),
-            dma((ITERS, 2)),
+            dma((ITERS,)),
+            dma((ITERS,)),
             dma((2,)),
             dma((2,)),
             dma((6,)),
             dma((6,)),
         ],
         compiler_params=pltpu.CompilerParams(
-            collective_id=0, has_side_effects=True, vmem_limit_bytes=48 * 1024 * 1024
+            collective_id=0, has_side_effects=True, vmem_limit_bytes=60 * 1024 * 1024
         ),
     )(student_feat, teacher_feat, prototypes, teacher_prototypes, live_count)
 

time: 97 us -> 93.6 us (0.965)
  local copies, waits for them, and re-layouts: 5.36 us -> 2.8 us
    unnamed x12 -> x2, local copies, waits for them, and re-layouts: 5.36 us -> 2.8 us
where the time goes in v2:
time: 93.6 us; the launch traced here: 93.4 us
  Pallas kernels  89.9 us (96%)
  local copies, waits for them, and re-layouts  2.8 us (3%)
    pallas_call x1, Pallas kernels, on_device(): pl.pallas_call(kernel, out_shape=(jax.ShapeDtypeStruct((SLOT, D), F32), j...  89.9 us
    unnamed x2, local copies, waits for them, and re-layouts  2.8 us

profile of v2, /device:TPU:1, one launch (start us, length us, event | category | flops | bytes accessed | tf_op | source)
XLA Modules:
  0.0 93.4 jit_solution(3120698732098826585)
XLA Ops:
  0.6 89.9 %shard_map.68 = (f32[12,256]{1,0:T(8,128)}, f32[1,64,256]{2,1,0:T(8,128)}) custom-call(bf16[12,256]{1,0:T(8,128)(2,1)} %sf_hbm.1, bf16[12,256]{1,0:T(8,128)(2,1)} %tf_hbm.1, bf16[1024,256]{1,0:T(8,128)(2,1)} %pr_hbm.1, bf16[1024,256]{1,0:T(8,128)(2,1)} %tp_hbm.1, s32[16]{0:T(128)} %lc_hbm.1), custom_call_target="tpu_custom_call" | custom-call | tf_op jit(solution)/shard_map/pallas_call | solution.py:334
  90.6 1.3 %copy.9 = f32[12,256]{1,0:T(8,128)} copy(f32[12,256]{1,0:T(8,128)} %get-tuple-element.4) | data formatting | bytes 24576
  91.9 1.5 %copy.10 = f32[1,64,256]{2,1,0:T(8,128)} copy(f32[1,64,256]{2,1,0:T(8,128)} %get-tuple-element.5) | data formatting | bytes 131072

commit v3 on v2

--- a/solution.py
+++ b/solution.py
@@ -51,7 +51,7 @@
     sf, tf, pr, tp, lc, isem,
     stage, msg, g1, trow, srow, tpb, prb, wt, ex, gr, ub, ab,
     cs, cr, rs, rr, ps, pg, vv,
-    pull, pullb, q1, q2s, q2, sixes, push, pushb, sib, zsend, zrecv,
+    pull, pullw, pullb, q1, q2s, q2, sixes, push, pushb, sib, zsend, zrecv,
     gsend, grecv, csend, crecv, rsend, rrecv, psend, precv, fsend, frecv,
 ):
     d = lax.axis_index("dp")
@@ -151,17 +151,25 @@
 
     second_gather(0, trow)
 
-    def scores(rows_ref, protos_ref, out_ref, scale):
-        for m in range(3):
-            for n in range(4):
+    def scores(rows_ref, protos_ref, out_ref, scale, weighted=False):
+        parts = []
+        for n in range(4):
+            acc = jnp.zeros((8, 256), F32)
+            for m in range(3):
                 rows, cols = pl.ds(m * 256, 256), pl.ds(n * 256, 256)
                 s = lax.dot_general(rows_ref[rows, :], protos_ref[cols, :], NT, preferred_element_type=F32)
-                out_ref[rows, cols] = jnp.exp(s * scale)
+                e = jnp.exp(s * scale)
+                out_ref[rows, cols] = e
+                if weighted:
+                    u = jnp.concatenate([ub[rows, :]] * 2, axis=1)
+                    acc = acc + jnp.sum((e * u).reshape(32, 8, 256), axis=0)
+            parts.append(acc)
+        return jnp.concatenate(parts, axis=1)
 
     wait(trow.at[pl.ds(0, 7 * CHUNK)], grecv.at[4])
     wait(trow.at[pl.ds(0, 7 * CHUNK)], grecv.at[5])
     second_gather(1, srow)
-    scores(trow, tpb, wt, 1.0 / 0.07)
+    first_sums = scores(trow, tpb, wt, 1.0 / 0.07, True)
 
     def column_pass(it):
         def body(i, acc):
@@ -173,7 +181,10 @@
                 acc = acc + w[t * 8 : t * 8 + 8] * ut
             return acc
 
-        acc = lax.fori_loop(0, ROWS // 32, body, jnp.zeros((8, PROTOS), F32), unroll=4)
+        if it == 0:
+            acc = first_sums
+        else:
+            acc = lax.fori_loop(0, ROWS // 32, body, jnp.zeros((8, PROTOS), F32), unroll=4)
         total = jnp.sum(acc, axis=0, keepdims=True)
         for n in range(8):
             cs[it, n : n + 1, :] = total[:, n * 128 : n * 128 + 128]
@@ -226,35 +237,39 @@
             partition = proto_sum(ps, pg, precv, 1)
             spread(10.0 * inverse(partition), ab)
 
+            v_row = jnp.concatenate([vv[n : n + 1, :] for n in range(8)], axis=1)
+
+            def by_protos(values):
+                high = values.astype(BF16)
+                low = (values - high.astype(F32)).astype(BF16)
+                return jnp.dot(high, prb[...], preferred_element_type=F32) + jnp.dot(
+                    low, prb[...], preferred_element_type=F32
+                )
+
             def fold(i, carry):
-                rows = pl.ds(pl.multiple_of(i * 32, 32), 32)
-                a = ab[rows, :]
-                for n in range(8):
-                    cols = pl.ds(n * 128, 128)
-                    ex[rows, cols] = ex[rows, cols] * a
-                    wt[rows, cols] = wt[rows, cols] * vv[n : n + 1, :]
+                rows = pl.ds(pl.multiple_of(i * 128, 128), 128)
+                e = ex[rows, :] * jnp.concatenate([ab[rows, :]] * 8, axis=1)
+                ex[rows, :] = e
+                pull[rows, :] = by_protos(e)
+                w = wt[rows, :] * v_row
+                wt[rows, :] = w
+                pullw[rows, :] = by_protos(w)
                 return carry
 
-            lax.fori_loop(0, ROWS // 32, fold, 0)
+            lax.fori_loop(0, ROWS // 128, fold, 0)
         wait(rr.at[it], rrecv.at[it])
         total = rs[it] + jnp.sum(rr[it], axis=0)
         spread(inverse(total) * (10.0 if it == ITERS - 1 else 1.0), ub)
 
-    def grads(i, carry):
-        rows = pl.ds(pl.multiple_of(i * 32, 32), 32)
-        u = ub[rows, :]
-        for n in range(8):
-            cols = pl.ds(n * 128, 128)
-            gr[rows, cols] = (ex[rows, cols] - wt[rows, cols] * u).astype(BF16)
-        return carry
-
-    lax.fori_loop(0, ROWS // 32, grads, 0)
-
-    for m in range(3):
-        rows = pl.ds(m * 256, 256)
-        part = jnp.dot(gr[rows, :], prb[...], preferred_element_type=F32)
+    def finish(i, carry):
+        rows = pl.ds(pl.multiple_of(i * 48, 48), 48)
+        u = jnp.concatenate([ub[rows, :]] * 2, axis=1)
+        part = pull[rows, :] - pullw[rows, :] * u
         pull[rows, :] = part
         pullb[rows, :] = part.astype(BF16)
+        return carry
+
+    lax.fori_loop(0, ROWS // 48, finish, 0, unroll=2)
     for k in FAR_FIRST:
         to_y = pl.ds(pl.multiple_of(((y + k) % NX) * CHUNK, CHUNK), CHUNK)
         to_x = pl.ds(pl.multiple_of(ROWS // 2 + ((x + k) % NX) * CHUNK, CHUNK), CHUNK)
@@ -263,8 +278,22 @@
 
     other = pl.ds(pl.multiple_of((1 - c) * 512, 512), 512)
     mine = pl.ds(pl.multiple_of(c * 512, 512), 512)
+
+    def grads(first):
+        def body(i, carry):
+            rows = pl.ds(pl.multiple_of(i * 32, 32), 32)
+            u = ub[rows, :]
+            for n in range(4):
+                cols = pl.ds(pl.multiple_of(first + n * 128, 128), 128)
+                gr[rows, cols] = (ex[rows, cols] - wt[rows, cols] * u).astype(BF16)
+            return carry
+
+        lax.fori_loop(0, ROWS // 32, body, 0, unroll=2)
+
+    grads((1 - c) * 512)
     pushb[...] = lax.dot_general(gr[:, other], srow[...], TN, preferred_element_type=F32).astype(BF16)
     send(pushb, sib, fsend.at[2], frecv.at[2], (z * 2 + 1 - c, p))
+    grads(c * 512)
     push[...] = lax.dot_general(gr[:, mine], srow[...], TN, preferred_element_type=F32)
     wait(sib, frecv.at[2])
     zsend[...] = (push[...] + sib[...].astype(F32)).astype(BF16).reshape(8, 64, D)
@@ -328,7 +357,7 @@
     wait(sib, fsend.at[2])
 
 
-def on_device(student_feat, teacher_feat, prototypes, teacher_prototypes, live_count):
+def on_device(*arguments):
     vmem = pl.BlockSpec(memory_space=pltpu.VMEM)
     dma = pltpu.SemaphoreType.DMA
     return pl.pallas_call(
@@ -337,7 +366,7 @@
             jax.ShapeDtypeStruct((SLOT, D), F32),
             jax.ShapeDtypeStruct((1, PROTOS // 16, D), F32),
         ),
-        in_specs=[pl.BlockSpec(memory_space=pl.ANY)] * 5,
+        in_specs=[pl.BlockSpec(memory_space=pltpu.HBM)] * 5,
         out_specs=(vmem, vmem),
         scratch_shapes=[
             pltpu.VMEM((SLOT, D), BF16),
@@ -366,6 +395,7 @@
             pltpu.VMEM((2, 7, 6, 128), F32),
             pltpu.VMEM((8, 128), F32),
             pltpu.VMEM((ROWS, D), F32),
+            pltpu.VMEM((ROWS, D), F32),
             pltpu.VMEM((ROWS, D), BF16),
             pltpu.VMEM((2, 7, CHUNK, D), BF16),
             pltpu.VMEM((2, NX, 8, D), F32),
@@ -388,9 +418,9 @@
             dma((6,)),
         ],
         compiler_params=pltpu.CompilerParams(
-            collective_id=0, has_side_effects=True, vmem_limit_bytes=60 * 1024 * 1024
+            collective_id=0, has_side_effects=True, vmem_limit_bytes=40 * 1024 * 1024
         ),
-    )(student_feat, teacher_feat, prototypes, teacher_prototypes, live_count)
+    )(*(pltpu.with_memory_space_constraint(a, pltpu.HBM) for a in arguments))
 
 
 def solution(mesh):

time: 93.6 us -> 91.2 us (0.974)
  local copies, waits for them, and re-layouts: 2.8 us -> 1.24 us
    unnamed x2, local copies, waits for them, and re-layouts: 2.8 us -> 1.24 us
where the time goes in v3:
time: 91.2 us; the launch traced here: 91 us
  Pallas kernels  89.2 us (98%)
  local copies, waits for them, and re-layouts  1.24 us (1%)
    pallas_call x1, Pallas kernels, on_device(): pl.pallas_call(kernel, out_shape=(jax.ShapeDtypeStruct((SLOT, D), F32), j...  89.2 us

profile of v3, /device:TPU:1, one launch (start us, length us, event | category | flops | bytes accessed | tf_op | source)
XLA Modules:
  0.0 91.0 jit_solution(11806206631707454250)
XLA Ops:
  0.6 89.2 %shard_map.68 = (f32[12,256]{1,0:T(8,128)S(1)}, f32[1,64,256]{2,1,0:T(8,128)S(1)}) custom-call(bf16[12,256]{1,0:T(8,128)(2,1)} %sf_hbm.1, bf16[12,256]{1,0:T(8,128)(2,1)} %tf_hbm.1, bf16[1024,256]{1,0:T(8,128)(2,1)} %pr_hbm.1, bf16[1024,256]{1,0:T(8,128)(2,1)} %tp_hbm.1, s32[16]{0:T(128)} %lc_hbm.1), custom_call_target="tpu_custom_call" | custom-call | tf_op jit(solution)/shard_map/pallas_call | solution.py:363
  89.8 0.6 copy.9
  90.4 0.6 copy.10

commit v4 on v3

--- a/solution.py
+++ b/solution.py
@@ -80,8 +80,9 @@
         pltpu.make_async_copy(ref, ref, sem).wait()
 
     barrier = pltpu.get_barrier_semaphore()
-    for k in PLANE:
-        pl.semaphore_signal(barrier, inc=1, device_id=plane(k), device_id_type=MESH)
+    for k in FAR_FIRST:
+        pl.semaphore_signal(barrier, inc=1, device_id=xp(k), device_id_type=MESH)
+        pl.semaphore_signal(barrier, inc=1, device_id=yp(k), device_id_type=MESH)
     for k in range(1, 16):
         pl.semaphore_signal(barrier, inc=1, device_id=dpp(k), device_id_type=MESH)
 
@@ -106,7 +107,7 @@
     for kind in range(2):
         g1[kind, 0, x] = msg[kind, 0]
         g1[kind, 1, y] = msg[kind, 1]
-    pl.semaphore_wait(barrier, NX * NX - 1 + 15)
+    pl.semaphore_wait(barrier, 2 * (NX - 1) + 15)
     for kind in range(2):
         for k in FAR_FIRST:
             for half, at, peer in ((0, x, xp), (1, y, yp)):
@@ -139,17 +140,23 @@
     first = pl.ds(pl.multiple_of(y * CHUNK, CHUNK), CHUNK)
     second = pl.ds(pl.multiple_of(ROWS // 2 + x * CHUNK, CHUNK), CHUNK)
 
-    def second_gather(kind, rows_ref):
-        for half, place, peer in ((0, first, yp), (1, second, xp)):
+    def assemble(kind, rows_ref):
+        for half, place in ((0, first), (1, second)):
             wait(g1.at[kind, half, pl.ds(0, NX - 1)], grecv.at[kind * 2 + half])
             picked = jnp.dot(pick, g1[kind, half].reshape(NX * 16, 128), preferred_element_type=F32).astype(BF16)
             rows_ref[place, 0:128] = picked[0:CHUNK]
             rows_ref[place, 128:D] = picked[CHUNK:]
-            for k in FAR_FIRST:
-                sem = 4 + kind * 2 + half
-                send(rows_ref.at[place], rows_ref.at[place], gsend.at[sem], grecv.at[sem], peer(k))
-
-    second_gather(0, trow)
+            if kind == 0:
+                second_gather(kind, rows_ref, half)
+
+    def second_gather(kind, rows_ref, half):
+        place, peer = ((first, yp), (second, xp))[half]
+        for k in FAR_FIRST:
+            sem = 4 + kind * 2 + half
+            send(rows_ref.at[place], rows_ref.at[place], gsend.at[sem], grecv.at[sem], peer(k))
+
+    assemble(0, trow)
+    assemble(1, srow)
 
     def scores(rows_ref, protos_ref, out_ref, scale, weighted=False):
         parts = []
@@ -168,7 +175,6 @@
 
     wait(trow.at[pl.ds(0, 7 * CHUNK)], grecv.at[4])
     wait(trow.at[pl.ds(0, 7 * CHUNK)], grecv.at[5])
-    second_gather(1, srow)
     first_sums = scores(trow, tpb, wt, 1.0 / 0.07, True)
 
     def column_pass(it):
@@ -220,6 +226,9 @@
 
     for it in range(ITERS):
         column_pass(it)
+        if it == 0:
+            second_gather(1, srow, 0)
+            second_gather(1, srow, 1)
         if it == 1:
             wait(srow.at[pl.ds(0, 7 * CHUNK)], grecv.at[6])
             wait(srow.at[pl.ds(0, 7 * CHUNK)], grecv.at[7])

time: 91.2 us -> 90 us (0.987)
  Pallas kernels: 89.2 us -> 88 us
    pallas_call x1, Pallas kernels: 89.2 us -> 88 us  [on_device(): pl.pallas_call(kernel, out_shape=(jax.ShapeDtypeStruct((SLOT, D), F32), j...]
where the time goes in v4:
time: 90 us; the launch traced here: 89.8 us
  Pallas kernels  88 us (98%)
  local copies, waits for them, and re-layouts  1.24 us (1%)
    pallas_call x1, Pallas kernels, on_device(): pl.pallas_call(kernel, out_shape=(jax.ShapeDtypeStruct((SLOT, D), F32), j...  88 us

profile of v4, /device:TPU:1, one launch (start us, length us, event | category | flops | bytes accessed | tf_op | source)
XLA Modules:
  0.0 89.8 jit_solution(6288252835517489294)
XLA Ops:
  0.6 88.0 %shard_map.68 = (f32[12,256]{1,0:T(8,128)S(1)}, f32[1,64,256]{2,1,0:T(8,128)S(1)}) custom-call(bf16[12,256]{1,0:T(8,128)(2,1)} %sf_hbm.1, bf16[12,256]{1,0:T(8,128)(2,1)} %tf_hbm.1, bf16[1024,256]{1,0:T(8,128)(2,1)} %pr_hbm.1, bf16[1024,256]{1,0:T(8,128)(2,1)} %tp_hbm.1, s32[16]{0:T(128)} %lc_hbm.1), custom_call_target="tpu_custom_call" | custom-call | tf_op jit(solution)/shard_map/pallas_call | solution.py:372
  88.6 0.6 copy.9
  89.2 0.6 copy.10

commit v5 on v4

--- a/solution.py
+++ b/solution.py
@@ -366,10 +366,21 @@
     wait(sib, fsend.at[2])
 
 
+def hand_out(rows, protos, out_s, out_p, sem):
+    copies = (
+        pltpu.make_async_copy(rows, out_s, sem.at[0]),
+        pltpu.make_async_copy(protos, out_p, sem.at[1]),
+    )
+    for copy in copies:
+        copy.start()
+    for copy in copies:
+        copy.wait()
+
+
 def on_device(*arguments):
     vmem = pl.BlockSpec(memory_space=pltpu.VMEM)
     dma = pltpu.SemaphoreType.DMA
-    return pl.pallas_call(
+    grads = pl.pallas_call(
         kernel,
         out_shape=(
             jax.ShapeDtypeStruct((SLOT, D), F32),
@@ -430,6 +441,17 @@
             collective_id=0, has_side_effects=True, vmem_limit_bytes=40 * 1024 * 1024
         ),
     )(*(pltpu.with_memory_space_constraint(a, pltpu.HBM) for a in arguments))
+    return pl.pallas_call(
+        hand_out,
+        out_shape=(
+            jax.ShapeDtypeStruct((SLOT, D), F32),
+            jax.ShapeDtypeStruct((1, PROTOS // 16, D), F32),
+        ),
+        in_specs=[vmem, vmem],
+        compiler_params=pltpu.CompilerParams(vmem_limit_bytes=1024 * 1024),
+        out_specs=(pl.BlockSpec(memory_space=pl.ANY),) * 2,
+        scratch_shapes=[dma((2,))],
+    )(*grads)
 
 
 def solution(mesh):

time: 90 us -> 89.4 us (level)
  local copies, waits for them, and re-layouts: 1.24 us -> 0 us
    unnamed x2 -> x0, local copies, waits for them, and re-layouts: 1.24 us -> none
where the time goes in v5:
time: 89.4 us; the launch traced here: 89.2 us
  Pallas kernels  88.6 us (99%)
    pallas_call x1, Pallas kernels, on_device(): pl.pallas_call(kernel, out_shape=(jax.ShapeDtypeStruct((SLOT, D), F32), j...  88 us

profile of v5, /device:TPU:1, one launch (start us, length us, event | category | flops | bytes accessed | tf_op | source)
XLA Modules:
  0.0 89.2 jit_solution(1847527467046020835)
XLA Ops:
  0.6 88.0 %shard_map.68 = (f32[12,256]{1,0:T(8,128)S(1)}, f32[1,64,256]{2,1,0:T(8,128)S(1)}) custom-call(bf16[12,256]{1,0:T(8,128)(2,1)} %sf_hbm.1, bf16[12,256]{1,0:T(8,128)(2,1)} %tf_hbm.1, bf16[1024,256]{1,0:T(8,128)(2,1)} %pr_hbm.1, bf16[1024,256]{1,0:T(8,128)(2,1)} %tp_hbm.1, s32[16]{0:T(128)} %lc_hbm.1), custom_call_target="tpu_custom_call" | custom-call | tf_op jit(solution)/shard_map/pallas_call | solution.py:383
  88.6 0.7 shard_map.69
